TPU v7x, 32 devices: a whole 2x2x4 slice. The times are simulated.
32 devices in a mesh: wide: 16 (over z, x, core), narrow: 2 (over y).
Axes of the slice: x: 2, y: 2, z: 4, core: 2. Of those that a mesh axis runs over, the one named last changes fastest.
Arguments:
- tokens: bfloat16 [16384, 768], P(('wide', 'narrow')), may hold values from -6 to 6
- cotangent: bfloat16 [16384, 768], P(('wide', 'narrow')), may hold values from -6 to 6
- w_in: bfloat16 [768, 2304], P(('wide', 'narrow')), may hold values from -0.21875 to 0.21875
- w_out: bfloat16 [768, 768], P(('wide', 'narrow')), may hold values from -0.4375 to 0.4375
- w_gu: bfloat16 [768, 6144], P(('wide', 'narrow')), may hold values from -0.21875 to 0.21875
- w_down: bfloat16 [3072, 768], P(('wide', 'narrow')), may hold values from -0.21875 to 0.21875
- gain_mix: bfloat16 [768], P(('wide', 'narrow')), may hold values from 0.3984375 to 1.59375
- gain_ffn: bfloat16 [768], P(('wide', 'narrow')), may hold values from 0.3984375 to 1.59375
- buckets: int32 [32], P(('wide', 'narrow')), may hold values from 0 to 2, as said below
- lengths: int32 [32, 4], P(('wide', 'narrow')), may hold values from 0 to 512, as said below
Outputs:
- layer_out: bfloat16 [16384, 768], P(('wide', 'narrow'))
- grad_tokens: bfloat16 [16384, 768], P(('wide', 'narrow'))
- grad_w_in: float32 [768, 2304], P(('wide', 'narrow'))
- grad_w_out: float32 [768, 768], P(('wide', 'narrow'))
- grad_w_gu: float32 [768, 6144], P(('wide', 'narrow'))
- grad_w_down: float32 [3072, 768], P(('wide', 'narrow'))
- grad_gain_mix: float32 [768], P(('wide', 'narrow'))
- grad_gain_ffn: float32 [768], P(('wide', 'narrow'))
- kernel_norms: float32 [768], P(('wide', 'narrow'))
Inputs may be any that keep to these rules, and one draw needn't show every extreme that they name: `buckets`: bucket of each device block: 0 holds 4 rows of 128 slots, 1 holds 2 rows of 256, 2 holds one row of 512; some block has bucket 2. `lengths`: valid slots at the front of each row of a block; row slots past the bucket's row count are 0; every used row is at least half valid and the first row of each block is fully valid.
All inputs are finite; a program needn't handle non-finite values.
Results may differ from a plain program's by a relative error of at most 0.018.
Values may be sent and summed in bfloat16 or wider, within the bound.
No kernel may reach another device: no remote copies, remote signals or barrier semaphores. Data moves between devices by JAX's collectives and lax.ppermute only.
A program may use at most 256 MiB of HBM per device.

v0:
```python
import math

import jax
import jax.numpy as jnp
from jax import lax
from jax.sharding import PartitionSpec as P

HIGHEST_PRECISION = lax.Precision.HIGHEST


def row_mask(bucket_id, length_row, tok_count):
    row_total = jnp.where(bucket_id == 0, 4, jnp.where(bucket_id == 1, 2, 1)).astype(jnp.int32)
    row_length = tok_count // row_total
    position = jnp.arange(tok_count, dtype=jnp.int32)
    slot_index = position // row_length
    within_row = position - slot_index * row_length
    slot_ids = jnp.arange(4, dtype=jnp.int32)
    length_here = jnp.sum(
        jnp.where(slot_index[:, None] == slot_ids[None, :], length_row[None, :], 0), axis=1
    )
    return (within_row < length_here).astype(jnp.float32)[:, None]


def rms_scale(values, gain):
    return values * lax.rsqrt(jnp.mean(values * values, axis=-1, keepdims=True) + 1e-06) * gain


def angle_table(size_left, size_right, period):
    product_index = (
        jnp.arange(size_left, dtype=jnp.int32)[:, None]
        * jnp.arange(size_right, dtype=jnp.int32)[None, :]
        % period
    )
    angles = product_index.astype(jnp.float32) * (2.0 * math.pi / period)
    return (jnp.cos(angles), jnp.sin(angles))


def split_length(length_total):
    first_size = math.gcd(length_total, 2 ** ((length_total.bit_length() - 1) // 2))
    return (first_size, length_total // first_size)


def forward_dft(signal_rows):
    row_total, length_total, channels = signal_rows.shape
    first_size, second_size = split_length(length_total)
    cos_first, sin_first = angle_table(first_size, first_size, first_size)
    cos_second, sin_second = angle_table(second_size, second_size, second_size)
    twist_cos, twist_sin = angle_table(first_size, second_size, length_total)
    twist_cos = twist_cos[None, :, :, None]
    twist_sin = twist_sin[None, :, :, None]
    grid_rows = signal_rows.reshape(row_total, first_size, second_size, channels)
    section_real = jnp.einsum("ka,rabc->rkbc", cos_first, grid_rows, precision=HIGHEST_PRECISION)
    section_imag = -jnp.einsum("ka,rabc->rkbc", sin_first, grid_rows, precision=HIGHEST_PRECISION)
    turned_real = section_real * twist_cos + section_imag * twist_sin
    turned_imag = section_imag * twist_cos - section_real * twist_sin
    spec_real = jnp.einsum(
        "rkbc,bm->rkmc", turned_real, cos_second, precision=HIGHEST_PRECISION
    ) + jnp.einsum("rkbc,bm->rkmc", turned_imag, sin_second, precision=HIGHEST_PRECISION)
    spec_imag = jnp.einsum(
        "rkbc,bm->rkmc", turned_imag, cos_second, precision=HIGHEST_PRECISION
    ) - jnp.einsum("rkbc,bm->rkmc", turned_real, sin_second, precision=HIGHEST_PRECISION)
    return (spec_real, spec_imag)


def inverse_dft(spec_real, spec_imag, length_total):
    row_total, first_size, second_size, channels = spec_real.shape
    cos_first, sin_first = angle_table(first_size, first_size, first_size)
    cos_second, sin_second = angle_table(second_size, second_size, second_size)
    twist_cos, twist_sin = angle_table(first_size, second_size, length_total)
    twist_cos = twist_cos[None, :, :, None]
    twist_sin = twist_sin[None, :, :, None]
    back_real = jnp.einsum(
        "rkmc,bm->rkbc", spec_real, cos_second, precision=HIGHEST_PRECISION
    ) - jnp.einsum("rkmc,bm->rkbc", spec_imag, sin_second, precision=HIGHEST_PRECISION)
    back_imag = jnp.einsum(
        "rkmc,bm->rkbc", spec_imag, cos_second, precision=HIGHEST_PRECISION
    ) + jnp.einsum("rkmc,bm->rkbc", spec_real, sin_second, precision=HIGHEST_PRECISION)
    untwist_real = back_real * twist_cos - back_imag * twist_sin
    untwist_imag = back_imag * twist_cos + back_real * twist_sin
    signal_grid = jnp.einsum(
        "ak,rkbc->rabc", cos_first, untwist_real, precision=HIGHEST_PRECISION
    ) - jnp.einsum("ak,rkbc->rabc", sin_first, untwist_imag, precision=HIGHEST_PRECISION)
    return (signal_grid / length_total).reshape(row_total, length_total, channels)


def conv_branch(row_total):

    def convolve(kernel, values):
        tok_count, model_width = kernel.shape
        row_length = tok_count // row_total
        kernel_rows = kernel.reshape(row_total, row_length, model_width)
        value_rows = values.reshape(row_total, row_length, model_width)
        squares = jnp.sum(kernel_rows * kernel_rows, axis=1, keepdims=True)
        norms = jnp.sqrt(squares + 1e-05)
        unit_rows = kernel_rows / norms
        kernel_real, kernel_imag = forward_dft(unit_rows)
        value_real, value_imag = forward_dft(value_rows)
        mixed_rows = inverse_dft(
            kernel_real * value_real - kernel_imag * value_imag,
            kernel_real * value_imag + kernel_imag * value_real,
            row_length,
        )
        return (mixed_rows.reshape(tok_count, model_width), jnp.mean(norms[:, 0, :], axis=0))

    return convolve


def product(left, right):
    return jnp.dot(left, right, preferred_element_type=jnp.float32)


def product_back(left, right):
    return lax.dot_general(
        left, right, (((1,), (1,)), ((), ())), preferred_element_type=jnp.float32
    )


def product_outer(left, right):
    return lax.dot_general(
        left, right, (((0,), (0,)), ((), ())), preferred_element_type=jnp.float32
    )


def on_device(tokens, cotangent, w_in, w_out, w_gu, w_down, gain_mix, gain_ffn, buckets, lengths):
    full_in, full_out, full_gu, full_down, gain_one_low, gain_two_low = (
        lax.all_gather(w_in, ("wide", "narrow"), axis=0, tiled=True),
        lax.all_gather(w_out, ("wide", "narrow"), axis=0, tiled=True),
        lax.all_gather(w_gu, ("wide", "narrow"), axis=0, tiled=True),
        lax.all_gather(w_down, ("wide", "narrow"), axis=0, tiled=True),
        lax.all_gather(gain_mix, ("wide", "narrow"), axis=0, tiled=True),
        lax.all_gather(gain_ffn, ("wide", "narrow"), axis=0, tiled=True),
    )
    gain_one = gain_one_low.astype(jnp.float32)
    gain_two = gain_two_low.astype(jnp.float32)
    bucket_id = buckets[0]
    pad_mask = row_mask(bucket_id, lengths[0], tokens.shape[0])
    activations = tokens.astype(jnp.float32)
    model_width = activations.shape[1]
    ff_width = full_down.shape[0]

    def mixer_local(projected):
        kernel = jnp.tanh(projected[:, :model_width]) * pad_mask
        gate_mix = projected[:, model_width : 2 * model_width]
        values = projected[:, 2 * model_width :] * pad_mask
        mixed_rows, norm_mean = lax.switch(
            bucket_id, [conv_branch(4), conv_branch(2), conv_branch(1)], kernel, values
        )
        return (mixed_rows * jax.nn.sigmoid(gate_mix) * pad_mask, norm_mean)

    def glu_local(gate_up):
        return jax.nn.silu(gate_up[:, :ff_width]) * gate_up[:, ff_width:]

    normed_float, norm_one_pull = jax.vjp(rms_scale, activations, gain_one)
    normed = normed_float.astype(jnp.bfloat16)
    projected = product(normed, full_in)
    gated_float, mixer_pull, norm_mean = jax.vjp(mixer_local, projected, has_aux=True)
    gated_mix = gated_float.astype(jnp.bfloat16)
    middle = activations + product(gated_mix, full_out)
    normed_ffn_float, norm_two_pull = jax.vjp(rms_scale, middle, gain_two)
    normed_ffn = normed_ffn_float.astype(jnp.bfloat16)
    gate_up = product(normed_ffn, full_gu)
    hidden_float, glu_pull = jax.vjp(glu_local, gate_up)
    hidden = hidden_float.astype(jnp.bfloat16)
    layer_out = ((middle + product(hidden, full_down)) * pad_mask).astype(jnp.bfloat16)
    back_in, back_out, back_gu, back_down = (
        lax.all_gather(w_in, ("wide", "narrow"), axis=0, tiled=True),
        lax.all_gather(w_out, ("wide", "narrow"), axis=0, tiled=True),
        lax.all_gather(w_gu, ("wide", "narrow"), axis=0, tiled=True),
        lax.all_gather(w_down, ("wide", "narrow"), axis=0, tiled=True),
    )
    grad_outer = cotangent.astype(jnp.float32) * pad_mask
    grad_ffn = grad_outer.astype(jnp.bfloat16)
    grad_down = product_outer(hidden, grad_ffn)
    grad_hidden = product_back(grad_ffn, back_down)
    (grad_gate_up,) = glu_pull(grad_hidden)
    grad_gate_low = grad_gate_up.astype(jnp.bfloat16)
    grad_gu = product_outer(normed_ffn, grad_gate_low)
    grad_normed_ffn = product_back(grad_gate_low, back_gu)
    grad_middle_part, grad_gain_two = norm_two_pull(grad_normed_ffn)
    grad_middle = grad_outer + grad_middle_part
    grad_mix = grad_middle.astype(jnp.bfloat16)
    grad_wout = product_outer(gated_mix, grad_mix)
    grad_gated = product_back(grad_mix, back_out)
    (grad_projected,) = mixer_pull(grad_gated)
    grad_proj_low = grad_projected.astype(jnp.bfloat16)
    grad_win = product_outer(normed, grad_proj_low)
    grad_normed = product_back(grad_proj_low, back_in)
    grad_input_part, grad_gain_one = norm_one_pull(grad_normed)
    grad_tokens = (grad_middle + grad_input_part).astype(jnp.bfloat16)
    wide_count = lax.axis_size("wide")
    narrow_count = lax.axis_size("narrow")

    def arrange(values):
        return values.reshape(
            (wide_count, narrow_count, values.shape[0] // (wide_count * narrow_count))
            + values.shape[1:]
        )

    def settle(values):
        return values.reshape(values.shape[2:])

    norm_term = norm_mean / lax.axis_size(("wide", "narrow"))
    norm_total = lax.psum(norm_term, ("wide", "narrow"))
    shard_width = model_width // lax.axis_size(("wide", "narrow"))
    kernel_norms = lax.dynamic_slice_in_dim(
        norm_total, lax.axis_index(("wide", "narrow")) * shard_width, shard_width, 0
    )
    part_win, part_wout, part_gu, part_down, part_gain_one, part_gain_two = (
        lax.psum_scatter(
            arrange(grad_win).astype(jnp.bfloat16), "narrow", scatter_dimension=1, tiled=True
        ).astype(jnp.float32),
        lax.psum_scatter(
            arrange(grad_wout).astype(jnp.bfloat16), "narrow", scatter_dimension=1, tiled=True
        ).astype(jnp.float32),
        lax.psum_scatter(
            arrange(grad_gu).astype(jnp.bfloat16), "narrow", scatter_dimension=1, tiled=True
        ).astype(jnp.float32),
        lax.psum_scatter(
            arrange(grad_down).astype(jnp.bfloat16), "narrow", scatter_dimension=1, tiled=True
        ).astype(jnp.float32),
        lax.psum_scatter(
            arrange(grad_gain_one).astype(jnp.bfloat16), "narrow", scatter_dimension=1, tiled=True
        ).astype(jnp.float32),
        lax.psum_scatter(
            arrange(grad_gain_two).astype(jnp.bfloat16), "narrow", scatter_dimension=1, tiled=True
        ).astype(jnp.float32),
    )
    sum_win, sum_wout, sum_gu, sum_down, sum_gain_one, sum_gain_two = (
        lax.psum_scatter(
            part_win.astype(jnp.bfloat16), "wide", scatter_dimension=0, tiled=True
        ).astype(jnp.float32),
        lax.psum_scatter(
            part_wout.astype(jnp.bfloat16), "wide", scatter_dimension=0, tiled=True
        ).astype(jnp.float32),
        lax.psum_scatter(
            part_gu.astype(jnp.bfloat16), "wide", scatter_dimension=0, tiled=True
        ).astype(jnp.float32),
        lax.psum_scatter(
            part_down.astype(jnp.bfloat16), "wide", scatter_dimension=0, tiled=True
        ).astype(jnp.float32),
        lax.psum_scatter(
            part_gain_one.astype(jnp.bfloat16), "wide", scatter_dimension=0, tiled=True
        ).astype(jnp.float32),
        lax.psum_scatter(
            part_gain_two.astype(jnp.bfloat16), "wide", scatter_dimension=0, tiled=True
        ).astype(jnp.float32),
    )
    return (
        layer_out,
        grad_tokens,
        settle(sum_win),
        settle(sum_wout),
        settle(sum_gu),
        settle(sum_down),
        settle(sum_gain_one),
        settle(sum_gain_two),
        kernel_norms,
    )


def solution(mesh):
    placed = (
        P(("wide", "narrow"), None),
        P(("wide", "narrow"), None),
        P(("wide", "narrow"), None),
        P(("wide", "narrow"), None),
        P(("wide", "narrow"), None),
        P(("wide", "narrow"), None),
        P(("wide", "narrow")),
        P(("wide", "narrow")),
        P(("wide", "narrow")),
        P(("wide", "narrow"), None),
    )
    return jax.shard_map(
        on_device,
        mesh=mesh,
        in_specs=placed,
        out_specs=(
            P(("wide", "narrow"), None),
            P(("wide", "narrow"), None),
            P(("wide", "narrow"), None),
            P(("wide", "narrow"), None),
            P(("wide", "narrow"), None),
            P(("wide", "narrow"), None),
            P(("wide", "narrow")),
            P(("wide", "narrow")),
            P(("wide", "narrow")),
        ),
        check_vma=False,
    )
```

profile of v0, /device:TPU:0, one launch (start us, length us, event | category | flops | bytes accessed | tf_op | source)
XLA Modules:
  0.0 1154.4 jit_solution(7554482717319786334)
XLA Ops:
  12.4 42.0 %all-reduce.13 = (bf16[768]{0:T(1024)(128)(2,1)S(1)}, bf16[768]{0:T(1024)(128)(2,1)S(1)}) all-reduce(bf16[768]{0:T(1024)(128)(2,1)S(1)} %dynamic-update-slice, bf16[768]{0:T(1024)(128)(2,1)S(1)} %dynamic-update-slice.1), channel_id=1, replica_groups=mesh['wide'=16,'narrow'=2] {'wide','narrow'}, use_global_device_ids=true, to_apply=%add.5 | all-reduce | flops 1536 | bytes 6144
  57.3 16.6 %all-gather.5.cloned.1.call-done = bf16[768,2304]{1,0:T(8,128)(2,1)} async-done(((bf16[24,2304]{1,0:T(8,128)(2,1)}), bf16[768,2304]{1,0:T(8,128)(2,1)}) %all-gather.5.cloned.1.call-update) | async-done | bytes 3538960 | tf_op jit(solution)/shard_map/all_gather | solution.py:126
  80.4 104.3 %conditional.2 = (f32[512,768]{1,0:T(8,128)}, f32[768]{0:T(1024)S(1)}, f32[4,128,768]{2,1,0:T(8,128)S(1)}, f32[4,1,768]{2,1,0:T(1,128)}, f32[4,1,768]{2,1,0:T(1,...) conditional(s32[]{:T(128)} %bitcast.286, ...), branch_computations={%region_2.5_spmd, %region_5.8_spmd, %region_8.10_spmd} | conditional | flops 2280294144 | bytes 118244408 | solution.py:145
  153.2 5.5 fusion.165
  158.7 5.7 multiply_bitcast_fusion.2
  190.6 23.2 %all-gather.9.cloned.1.call-done = bf16[768,6144]{1,0:T(8,128)(2,1)} async-done(((bf16[24,6144]{1,0:T(8,128)(2,1)}), bf16[768,6144]{1,0:T(8,128)(2,1)}) %all-gather.9.cloned.1.call-update) | async-done | bytes 9437200 | tf_op jit(solution)/shard_map/all_gather | solution.py:128
  213.7 11.7 %fusion.593 = f32[512,6144]{1,0:T(8,128)} fusion(bf16[768,6144]{1,0:T(8,128)(2,1)} %all-gather.9.cloned.1.call-done, f32[512,768]{1,0:T(8,128)S(1)} %get-tuple-element.734, f32[768]{0:T(1024)S(1)} %convert_element_type.401, f32[512]{0:T(512)S(1)} %fusion.586), kind=kOutput, calls=%fused_computation.792 | convolution fusion | flops 4833017856 | bytes 23598080 | tf_op jit(solution)/shard_map/dot_general | solution.py:109
  225.4 53.3 %all-gather.11.cloned.1.call-done = bf16[3072,768]{1,0:T(8,128)(2,1)} async-done(((bf16[96,768]{1,0:T(8,128)(2,1)}), bf16[3072,768]{1,0:T(8,128)(2,1)}) %all-gather.11.cloned.1.call-update) | async-done | bytes 4718608 | tf_op jit(solution)/shard_map/all_gather | solution.py:129
  278.8 12.5 %fusion.574 = (f32[512,3072]{1,0:T(8,128)}, f32[512,3072]{1,0:T(8,128)}, bf16[512,3072]{1,0:T(8,128)(2,1)}) fusion(f32[512,6144]{1,0:T(8,128)} %fusion.593, bf16[3072,768]{1,0:T(8,128)(2,1)} %all-gather.11.cloned.1.call-done, bf16[512,768]{1,0:T(8,128)(2,1)} %param.17, f32[512]{0:T(512)S(1)} %fusion.584), kind=kOutput, calls=%fused_computation.756 | convolution fusion | flops 2439118848 | bytes 33818624 | tf_op jit(solution)/shard_map/dot_general | solution.py:113
  291.2 12.3 %convolution_convert_fusion = bf16[768,6144]{1,0:T(8,128)(2,1)} fusion(f32[512,3072]{1,0:T(8,128)} %get-tuple-element.725, f32[512,3072]{1,0:T(8,128)} %get-tuple-element.724, f32[512,768]{1,0:T(8,128)S(1)} %get-tuple-element.734, f32[768]{0:T(1024)S(1)} %convert_element_type.401, f32[512]{0:T(512)S(1)} %fusion.586), kind=kOutput, calls=%fused_computation.708 | convolution fusion | flops 4844027904 | bytes 23598080 | tf_op jit(solution)/shard_map/dot_general | solution.py:119
  303.5 12.4 %multiply_reduce_fusion.4 = (bf16[768]{0:T(1024)(128)(2,1)}, f32[512]{0:T(512)S(1)}, f32[512,768]{1,0:T(8,128)}) fusion(f32[512,768]{1,0:T(8,128)S(1)} %get-tuple-element.734, f32[512]{0:T(512)S(1)} %fusion.586, f32[768]{0:T(1024)S(1)} %convert_element_type.401, bf16[768,6144]{1,0:T(8,128)(2,1)} %all-gather.9.cloned.1.call-done, ...), kind=kOutput, calls=%fused_computation.742 | convolution fusion | flops 4840487424 | bytes 25174528 | tf_op jit(solution)/shard_map/dot_general | solution.py:113
  329.9 88.4 %conditional.3 = (f32[512,768]{1,0:T(8,128)S(1)}, f32[512,768]{1,0:T(8,128)S(1)}) conditional(s32[]{:T(128)} %bitcast.286, (f32[512,768]{1,0:T(8,128)}, f32[8,8]{1,0:T(8,128)S(1)}, f32[1,8,16,1]{3,2,1,0:T(8,128)}, f32[8,8]{1,0:T(8,128)S(1)}, f32[1,8,16,1]{3,2,1,0:T(8,128)S(1)}, /*index=5*/f32[16,16]{1,0:T(8,128)S(1)}, ...), branch_computations={%region_12.14_spmd, %region_14.16_spmd, %region_16.18_spmd} | conditional | flops 2289697536 | bytes 122840592 | solution.py:145
  372.8 6.3 fusion.499
  396.3 5.8 add_bitcast_fusion.17
  411.8 5.4 add_bitcast_fusion.16
  426.5 6.8 fusion.561
  434.1 418.7 %all-reduce.18.cloned.1.call-done = (bf16[16,2,24,2304]{3,2,1,0:T(8,128)(2,1)}, bf16[16,2,24,768]{3,2,1,0:T(8,128)(2,1)}, bf16[16,2,24,6144]{3,2,1,0:T(8,128)(2,1)}, bf16[16,2,96,768]{3,2,1,0:T(8,128)(2,1)}) async-done(((bf16[16,2,24,2304]{3,2,1,0:T(8,128)(2,1)}, bf16[16,2,24,768]{3,2,1,0:T(8,128)(2,1)}, bf16[16,2,24,6144]{3,2,1,0:T(8,128)(2,1)}, bf16[16,2,96,768]{3,2,1,0:T(8,128)(2,1)}), ...) | async-done | bytes 18874384
  863.0 5.7 constant_dynamic-slice_fusion.3
  869.9 40.4 %psum.7 = f32[768]{0:T(1024)S(1)} all-reduce(f32[768]{0:T(1024)S(1)} %broadcast_multiply_fusion.6), channel_id=1, replica_groups=mesh['wide'=16,'narrow'=2] {'wide','narrow'}, use_global_device_ids=true, to_apply=%region_33.34 | all-reduce | flops 768 | bytes 6144 | tf_op jit(solution)/shard_map/psum | solution.py:203
  913.8 5.9 multiply_convert_fusion.1
  921.1 59.4 %all-reduce.14 = (bf16[16,1,24]{2,1,0:T(2,128)(2,1)S(1)}, bf16[16,1,24]{2,1,0:T(2,128)(2,1)S(1)}) all-reduce(bf16[16,1,24]{2,1,0:T(2,128)(2,1)S(1)} %copy.830, bf16[16,1,24]{2,1,0:T(2,128)(2,1)S(1)} %copy.832), channel_id=11, replica_groups=mesh['wide'=16,'narrow'=2] {'wide'}, use_global_device_ids=true, to_apply=%region_29.30.clone | all-reduce | flops 768 | bytes 3072
  983.0 18.2 %reduce-scatter.13.cloned.1.call-done = bf16[1,1,24,2304]{3,2,1,0:T(8,128)(2,1)} async-done(((bf16[16,1,24,2304]{3,2,1,0:T(8,128)(2,1)}), bf16[1,1,24,2304]{3,2,1,0:T(8,128)(2,1)}) %reduce-scatter.13.cloned.1.call-update) | async-done | bytes 110608 | tf_op jit(solution)/shard_map/reduce_scatter | solution.py:229
  1002.8 64.0 %reduce-scatter.19.cloned.1.call-done = bf16[1,1,96,768]{3,2,1,0:T(8,128)(2,1)} async-done(((bf16[16,1,96,768]{3,2,1,0:T(8,128)(2,1)}), bf16[1,1,96,768]{3,2,1,0:T(8,128)(2,1)}) %reduce-scatter.19.cloned.1.call-update) | async-done | bytes 147472 | tf_op jit(solution)/shard_map/reduce_scatter | solution.py:238
  1068.5 77.3 %reduce-scatter.17.cloned.1.call-done = bf16[1,1,24,6144]{3,2,1,0:T(8,128)(2,1)} async-done(((bf16[16,1,24,6144]{3,2,1,0:T(8,128)(2,1)}), bf16[1,1,24,6144]{3,2,1,0:T(8,128)(2,1)}) %reduce-scatter.17.cloned.1.call-update) | async-done | bytes 294928 | tf_op jit(solution)/shard_map/reduce_scatter | solution.py:235
  (221 shorter events, 177.1 us)
Async XLA Ops:
  7.2 66.7 %all-gather.5.cloned.1.call-start = ((), (), s32[]{:S(2)}) async-start(), calls=%async_computation.6 | async-start | bytes 3649536 | tf_op jit(solution)/shard_map/all_gather | solution.py:126
  7.9 180.0 %all-gather.7.cloned.1.call-start = ((), (), s32[]{:S(2)}) async-start(), calls=%async_computation.7 | async-start | bytes 1216512 | tf_op jit(solution)/shard_map/all_gather | solution.py:127
  8.7 205.1 %all-gather.9.cloned.1.call-start = ((), (), s32[]{:S(2)}) async-start(), calls=%async_computation.8 | async-start | bytes 9732096 | tf_op jit(solution)/shard_map/all_gather | solution.py:128
  9.4 269.4 %all-gather.11.cloned.1.call-start = ((), (), s32[]{:S(2)}) async-start(), calls=%async_computation.9 | async-start | bytes 4866048 | tf_op jit(solution)/shard_map/all_gather | solution.py:129
  10.0 842.8 %all-reduce.18.cloned.1.call-start = ((), (), s32[]{:S(2)}) async-start(), calls=%async_computation.16 | async-start | bytes 37748736
  54.4 23.8 %copy-start.29 = (f32[768]{0:T(1024)}, f32[768]{0:T(1024)S(1)}, u32[]{:S(2)}) copy-start(f32[768]{0:T(1024)S(1)} %convert_element_type.397) | copy-start | bytes 9220
  57.2 21.0 %copy-start.33 = (f32[512]{0:T(512)}, f32[512]{0:T(512)S(1)}, u32[]{:S(2)}) copy-start(f32[512]{0:T(512)S(1)} %fusion.585) | copy-start | bytes 6148
  107.0 8.1 copy-start.21
  108.8 44.3 %copy-start.6 = (f32[16,16]{1,0:T(8,128)}, f32[16,16]{1,0:T(8,128)S(1)}, u32[]{:S(2)}) copy-start(f32[16,16]{1,0:T(8,128)S(1)} %get-tuple-element.830) | copy-start | bytes 3076 | tf_op jit(solution)/shard_map/jvp()/cond
  108.9 49.8 %copy-start.2 = (f32[16,16]{1,0:T(8,128)}, f32[16,16]{1,0:T(8,128)S(1)}, u32[]{:S(2)}) copy-start(f32[16,16]{1,0:T(8,128)S(1)} %get-tuple-element.829) | copy-start | bytes 3076 | tf_op jit(solution)/shard_map/jvp()/cond
  109.0 41.3 %copy-start.16 = (f32[32,32]{1,0:T(8,128)}, f32[32,32]{1,0:T(8,128)S(1)}, u32[]{:S(2)}) copy-start(f32[32,32]{1,0:T(8,128)S(1)} %get-tuple-element.853) | copy-start | bytes 12292 | tf_op jit(solution)/shard_map/jvp()/cond
  109.0 42.7 %copy-start.14 = (f32[32,32]{1,0:T(8,128)}, f32[32,32]{1,0:T(8,128)S(1)}, u32[]{:S(2)}) copy-start(f32[32,32]{1,0:T(8,128)S(1)} %get-tuple-element.854) | copy-start | bytes 12292 | tf_op jit(solution)/shard_map/jvp()/cond
  190.5 113.0 %copy-start.9 = (f32[512,768]{1,0:T(8,128)}, f32[512,768]{1,0:T(8,128)S(1)}, u32[]{:S(2)}) copy-start(f32[512,768]{1,0:T(8,128)S(1)} %get-tuple-element.734) | copy-start | bytes 4718596
  315.9 4.6 copy-start.40
  320.6 4.7 copy-start.36
  325.3 4.6 copy-start.7
  325.3 4.6 copy-start.31
  424.5 495.2 %reduce-scatter.23.cloned.1.call-start = ((), (), s32[]{:S(2)}) async-start(), calls=%async_computation.15 | async-start | bytes 12288 | tf_op jit(solution)/shard_map/reduce_scatter | solution.py:224
  426.4 494.0 %reduce-scatter.21.cloned.1.call-start = ((), (), s32[]{:S(2)}) async-start(), calls=%async_computation.14 | async-start | bytes 12288 | tf_op jit(solution)/shard_map/reduce_scatter | solution.py:221
  434.0 547.6 %reduce-scatter.15.cloned.1.call-start = ((), (), s32[]{:S(2)}) async-start(), calls=%async_computation.11 | async-start | bytes 626688 | tf_op jit(solution)/shard_map/reduce_scatter | solution.py:232
  855.4 145.9 %reduce-scatter.13.cloned.1.call-start = ((), (), s32[]{:S(2)}) async-start(), calls=%async_computation.10 | async-start | bytes 1880064 | tf_op jit(solution)/shard_map/reduce_scatter | solution.py:229
  859.0 207.9 %reduce-scatter.19.cloned.1.call-start = ((), (), s32[]{:S(2)}) async-start(), calls=%async_computation.13 | async-start | bytes 2506752 | tf_op jit(solution)/shard_map/reduce_scatter | solution.py:238
  863.0 282.8 %reduce-scatter.17.cloned.1.call-start = ((), (), s32[]{:S(2)}) async-start(), calls=%async_computation.12 | async-start | bytes 5013504 | tf_op jit(solution)/shard_map/reduce_scatter | solution.py:235
  868.7 42.2 %copy-start.28 = (f32[512]{0:T(512)S(1)}, f32[512]{0:T(512)}, u32[]{:S(2)}) copy-start(f32[512]{0:T(512)} %copy-done.27) | copy-start | bytes 6148
  (23 other events, 49.4 us)
Sparse Core Ops, SparseCore 0:
  10.9 62.9 all-gather.4
  76.8 52.9 all-gather.6
  132.7 80.9 all-gather.8
  216.5 62.2 all-gather.10
  424.6 428.0 all-reduce.17
  855.5 10.7 reduce-scatter.22
  869.1 9.7 reduce-scatter.20
  883.4 54.7 reduce-scatter.14
  942.0 59.1 reduce-scatter.12
  1004.8 61.9 reduce-scatter.18
  1071.2 74.5 reduce-scatter.16
where the time goes:
time: 1160 us; the launch traced here: 1150 us
  waiting for transfers between devices  674 us (58%)
  matrix products  188 us (16%)
  blocking collectives  142 us (12%)
  loops' own time  53.2 us (5%)
  local copies, waits for them, and re-layouts  51.2 us (4%)
  other arithmetic  30.3 us (3%)
  between operations  15.1 us (1%)
    unnamed x12, waiting for transfers between devices  421 us
    unnamed x2, blocking collectives  101 us
    reduce_scatter x1, waiting for transfers between devices, on_device(): lax.psum_scatter(part_gu.astype(jnp.bfloat16), 'wide', scatter_dimension=...  77.3 us
    reduce_scatter x1, waiting for transfers between devices, on_device(): lax.psum_scatter(part_down.astype(jnp.bfloat16), 'wide', scatter_dimensio...  64 us
    all_gather x1, waiting for transfers between devices, on_device(): lax.all_gather(w_down, ('wide', 'narrow'), axis=0, tiled=True)  53.3 us
    another operation x2, loops' own time, mixer_local(): lax.switch(bucket_id, [conv_branch(4), conv_branch(2), conv_branch(1)], k...  53.2 us
    psum x1, blocking collectives, on_device(): norm_total = lax.psum(norm_term, ('wide', 'narrow'))  40.4 us
    dot_general x4, matrix products, product_back(): lax.dot_general(left, right, (((1,), (1,)), ((), ())), preferred_element_...  36.3 us
  transfers between devices with their start and end apart: 11, of which 7 were waited for; matrix products, arithmetic and copies ran while one was open for 13% of the time, Pallas kernels for 0%

commit v1 on v0

v1 whole, which is shorter than its diff:
```python
import functools

import jax
import jax.numpy as jnp
import ml_dtypes
import numpy as np
from jax import lax
from jax.experimental import pallas as pl
from jax.experimental.pallas import tpu as pltpu
from jax.sharding import PartitionSpec as P

F32 = jnp.float32
BF16 = jnp.bfloat16
ROW_SLOTS = 4
BUCKETS = 3
VMEM_BYTES = 56 * 1024 * 1024


def transform_tables(tok_count):
    highs, lows = [], []
    for bucket in range(BUCKETS):
        rows = ROW_SLOTS >> bucket
        length = tok_count // rows
        half = length // 2
        angle = 2.0 * np.pi * (np.arange(half)[:, None] * np.arange(length)[None, :] % length) / length
        real = np.cos(angle) * np.sqrt(2.0 / length)
        imag = -np.sin(angle) * np.sqrt(2.0 / length)
        real[0] = 1.0 / np.sqrt(length)
        imag[0] = (1.0 - 2.0 * (np.arange(length) % 2)) / np.sqrt(length)
        table = np.zeros((tok_count, tok_count))
        for row in range(rows):
            at = slice(row * length, (row + 1) * length)
            table[row * half : (row + 1) * half, at] = real
            table[tok_count // 2 + row * half : tok_count // 2 + (row + 1) * half, at] = imag
        high = table.astype(ml_dtypes.bfloat16)
        highs.append(high)
        lows.append((table - high.astype(np.float64)).astype(ml_dtypes.bfloat16))
    high, low = np.stack(highs), np.stack(lows)
    return high, low, np.ascontiguousarray(high.transpose(0, 2, 1)), np.ascontiguousarray(low.transpose(0, 2, 1))


def mm(left, right):
    return jnp.dot(left, right, preferred_element_type=F32)


def mm_nt(left, right):
    return lax.dot_general(left, right, (((1,), (1,)), ((), ())), preferred_element_type=F32)


def mm_tn(left, right):
    return lax.dot_general(left, right, (((0,), (0,)), ((), ())), preferred_element_type=F32)


def transform(high, low, values):
    top = values.astype(BF16)
    rest = (values - top.astype(F32)).astype(BF16)
    return mm(high, top) + (mm(high, rest) + mm(low, top))


def bin_facts(bucket, shape, tok_count):
    half = lax.shift_left(jnp.int32(tok_count // (2 * ROW_SLOTS)), bucket)
    spot = lax.broadcasted_iota(jnp.int32, shape, 0)
    edge = (spot & (half - 1)) == 0
    length = (2 * half).astype(F32)
    scale = jnp.where(edge, jnp.sqrt(length), jnp.sqrt(0.5 * length))
    return edge, scale


def pad_mask(bucket, lengths, shape, tok_count):
    quarter = tok_count // ROW_SLOTS
    shift = (quarter.bit_length() - 1) + bucket
    spot = lax.broadcasted_iota(jnp.int32, shape, 0)
    slot = lax.shift_right_logical(spot, jnp.broadcast_to(shift, shape))
    within = spot - lax.shift_left(slot, jnp.broadcast_to(shift, shape))
    length = jnp.where(
        slot == 0, lengths[0], jnp.where(slot == 1, lengths[1], jnp.where(slot == 2, lengths[2], lengths[3]))
    )
    return (within < length).astype(F32)


def row_sums(bucket, values, tok_count):
    quarter = tok_count // ROW_SLOTS
    s = [jnp.sum(values[i * quarter : (i + 1) * quarter], axis=0, keepdims=True) for i in range(ROW_SLOTS)]
    left, right = s[0] + s[1], s[2] + s[3]
    whole = left + right
    pairs = (left, left, right, right)
    return [jnp.where(bucket == 0, s[i], jnp.where(bucket == 1, pairs[i], whole)) for i in range(ROW_SLOTS)]


def over_rows(parts, tok_count):
    quarter = tok_count // ROW_SLOTS
    return jnp.concatenate([jnp.broadcast_to(p, (quarter, p.shape[1])) for p in parts], axis=0)


def mix_forward_kernel(
    facts, x_ref, g1_ref, g2_ref, wa_ref, wc_ref, wv_ref, wo_ref, mh_ref, ml_ref, th_ref, tl_ref,
    normed_ref, gated_ref, mid_ref, nf_ref, t_ref, s_ref, mix_ref, kf_ref, vf_ref, norm_ref, acc_ref,
):
    step = pl.program_id(0)
    tok_count = x_ref.shape[0]
    bucket = facts[0]
    lengths = [facts[1 + i] for i in range(ROW_SLOTS)]

    @pl.when(step == 0)
    def _():
        x = x_ref[...].astype(F32)
        r = lax.rsqrt(jnp.mean(x * x, axis=-1, keepdims=True) + 1e-06)
        normed_ref[...] = (x * r * g1_ref[...]).astype(BF16)

    normed = normed_ref[...]
    a = mm(normed, wa_ref[...])
    c = mm(normed, wc_ref[...])
    v = mm(normed, wv_ref[...])
    mask = pad_mask(bucket, lengths, a.shape, tok_count)
    t = jnp.tanh(a) * mask
    v = v * mask
    squares = [s + 1e-05 for s in row_sums(bucket, t * t, tok_count)]
    norms = [jnp.sqrt(s) for s in squares]
    norm_ref[...] = (norms[0] + norms[1] + norms[2] + norms[3]) * 0.25
    unit = t * over_rows([1.0 / n for n in norms], tok_count)
    half = tok_count // 2
    kf = transform(mh_ref[0], ml_ref[0], unit)
    vf = transform(mh_ref[0], ml_ref[0], v)
    kf_ref[...] = kf
    vf_ref[...] = vf
    edge, scale = bin_facts(bucket, (half, a.shape[1]), tok_count)
    kr, ki, vr, vi = kf[:half], kf[half:], vf[:half], vf[half:]
    kivi = ki * vi
    pr = (kr * vr - jnp.where(edge, 0.0, kivi)) * scale
    pi = jnp.where(edge, kivi, kr * vi + ki * vr) * scale
    mixed = transform(th_ref[0], tl_ref[0], jnp.concatenate([pr, pi], axis=0))
    sig = 1.0 / (1.0 + jnp.exp(-c))
    t_ref[...] = t
    s_ref[...] = sig
    mix_ref[...] = mixed
    gated = (mixed * sig * mask).astype(BF16)
    gated_ref[...] = gated
    part = mm(gated, wo_ref[...])

    @pl.when(step == 0)
    def _():
        acc_ref[...] = part

    @pl.when(step > 0)
    def _():
        acc_ref[...] += part

    @pl.when(step == pl.num_programs(0) - 1)
    def _():
        mid = x_ref[...].astype(F32) + acc_ref[...]
        mid_ref[...] = mid
        r = lax.rsqrt(jnp.mean(mid * mid, axis=-1, keepdims=True) + 1e-06)
        nf_ref[...] = (mid * r * g2_ref[...]).astype(BF16)


def mix_forward(facts, x, g1, g2, half0, half1, tables):
    tok, width = x.shape
    tile = 256
    steps = width // tile
    whole = lambda shape: pl.BlockSpec(shape, lambda j, s: (0,) * len(shape))
    table = pl.BlockSpec((1, tok, tok), lambda j, s: (s[0], 0, 0))
    column = pl.BlockSpec((tok, tile), lambda j, s: (0, j))
    return pl.pallas_call(
        mix_forward_kernel,
        grid_spec=pltpu.PrefetchScalarGridSpec(
            num_scalar_prefetch=1,
            grid=(steps,),
            in_specs=[
                whole((tok, width)), whole((1, width)), whole((1, width)),
                pl.BlockSpec((width, tile), lambda j, s: (0, j)),
                pl.BlockSpec((width, tile), lambda j, s: (0, steps + j)),
                pl.BlockSpec((width, tile), lambda j, s: (0, j)),
                pl.BlockSpec((tile, width), lambda j, s: (j, 1)),
                table, table, table, table,
            ],
            out_specs=[
                whole((tok, width)), column, whole((tok, width)), whole((tok, width)),
                column, column, column, column, column,
                pl.BlockSpec((1, tile), lambda j, s: (0, j)),
            ],
            scratch_shapes=[pltpu.VMEM((tok, width), F32)],
        ),
        out_shape=[
            jax.ShapeDtypeStruct((tok, width), BF16), jax.ShapeDtypeStruct((tok, width), BF16),
            jax.ShapeDtypeStruct((tok, width), F32), jax.ShapeDtypeStruct((tok, width), BF16),
            *[jax.ShapeDtypeStruct((tok, width), F32)] * 5,
            jax.ShapeDtypeStruct((1, width), F32),
        ],
        compiler_params=pltpu.CompilerParams(vmem_limit_bytes=VMEM_BYTES),
        name="mix_forward",
    )(facts, x, g1, g2, half0, half0, half1, half1, *tables)


def rms_back(values, gain, grad):
    r = lax.rsqrt(jnp.mean(values * values, axis=-1, keepdims=True) + 1e-06)
    scaled = values * r
    inner = grad * gain
    dot = jnp.mean(inner * scaled, axis=-1, keepdims=True)
    return r * (inner - scaled * dot), grad * scaled


def mix_back_kernel(
    facts, x_ref, cot_ref, g1_ref, g2_ref, mid_ref, own_ref, sib_ref, normed_ref, gated_ref,
    t_ref, s_ref, mix_ref, kf_ref, vf_ref, wa_ref, wc_ref, wv_ref, wo_ref, mh_ref, ml_ref, th_ref, tl_ref,
    tok_ref, ga_ref, gc_ref, gv_ref, go_ref, gain1_ref, gain2_ref, gm_ref, low_ref, acc_ref,
):
    step = pl.program_id(0)
    tok_count = x_ref.shape[0]
    bucket = facts[0]
    lengths = [facts[1 + i] for i in range(ROW_SLOTS)]

    @pl.when(step == 0)
    def _():
        outer = cot_ref[...].astype(F32) * pad_mask(bucket, lengths, cot_ref.shape, tok_count)
        grad = own_ref[...] + sib_ref[...].astype(F32)
        back, terms = rms_back(mid_ref[...], g2_ref[...], grad)
        gain2_ref[...] = jnp.sum(terms, axis=0, keepdims=True)
        grad_mid = outer + back
        gm_ref[...] = grad_mid
        low_ref[...] = grad_mid.astype(BF16)

    low = low_ref[...]
    grad_gated = mm_nt(low, wo_ref[...])
    go_ref[...] = mm_tn(gated_ref[...], low).astype(BF16)
    mask = pad_mask(bucket, lengths, grad_gated.shape, tok_count)
    grad_gated = grad_gated * mask
    sig = s_ref[...]
    grad_c = grad_gated * mix_ref[...] * (sig * (1.0 - sig))
    half = tok_count // 2
    df = transform(mh_ref[0], ml_ref[0], grad_gated * sig)
    edge, scale = bin_facts(bucket, (half, sig.shape[1]), tok_count)
    kf, vf = kf_ref[...], vf_ref[...]
    kr, ki, vr, vi = kf[:half], kf[half:], vf[:half], vf[half:]
    dr, di = df[:half] * scale, df[half:] * scale
    divi, diki = di * vi, di * ki
    dkr = dr * vr + jnp.where(edge, 0.0, divi)
    dki = jnp.where(edge, divi, di * vr - dr * vi)
    dvr = dr * kr + jnp.where(edge, 0.0, diki)
    dvi = jnp.where(edge, diki, di * kr - dr * ki)
    du = transform(th_ref[0], tl_ref[0], jnp.concatenate([dkr, dki], axis=0))
    dv = transform(th_ref[0], tl_ref[0], jnp.concatenate([dvr, dvi], axis=0)) * mask
    t = t_ref[...]
    inverse = [lax.rsqrt(s + 1e-05) for s in row_sums(bucket, t * t, tok_count)]
    dots = row_sums(bucket, du * t, tok_count)
    coupling = [d * i * i * i for d, i in zip(dots, inverse)]
    dt = du * over_rows(inverse, tok_count) - t * over_rows(coupling, tok_count)
    da = (dt * mask * (1.0 - t * t)).astype(BF16)
    dc = grad_c.astype(BF16)
    dv = dv.astype(BF16)
    normed = normed_ref[...]
    ga_ref[...] = mm_tn(normed, da).astype(BF16)
    gc_ref[...] = mm_tn(normed, dc).astype(BF16)
    gv_ref[...] = mm_tn(normed, dv).astype(BF16)
    part = mm_nt(da, wa_ref[...]) + mm_nt(dc, wc_ref[...]) + mm_nt(dv, wv_ref[...])

    @pl.when(step == 0)
    def _():
        acc_ref[...] = part

    @pl.when(step > 0)
    def _():
        acc_ref[...] += part

    @pl.when(step == pl.num_programs(0) - 1)
    def _():
        back, terms = rms_back(x_ref[...].astype(F32), g1_ref[...], acc_ref[...])
        gain1_ref[...] = jnp.sum(terms, axis=0, keepdims=True)
        tok_ref[...] = (gm_ref[...] + back).astype(BF16)


def mix_back(facts, x, cot, g1, g2, mid, own, sib, normed, gated, kept, half0, half1, tables):
    tok, width = x.shape
    tile = 256
    steps = width // tile
    whole = lambda shape: pl.BlockSpec(shape, lambda j, s: (0,) * len(shape))
    table = pl.BlockSpec((1, tok, tok), lambda j, s: (s[0], 0, 0))
    column = pl.BlockSpec((tok, tile), lambda j, s: (0, j))
    tall = pl.BlockSpec((width, tile), lambda j, s: (0, j))
    rows = (tok, width)
    return pl.pallas_call(
        mix_back_kernel,
        grid_spec=pltpu.PrefetchScalarGridSpec(
            num_scalar_prefetch=1,
            grid=(steps,),
            in_specs=[
                whole(rows), whole(rows), whole((1, width)), whole((1, width)), whole(rows), whole(rows), whole(rows),
                whole(rows), column, column, column, column, column, column,
                tall,
                pl.BlockSpec((width, tile), lambda j, s: (0, steps + j)),
                tall,
                pl.BlockSpec((tile, width), lambda j, s: (j, 1)),
                table, table, table, table,
            ],
            out_specs=[
                whole(rows), tall, tall, tall,
                pl.BlockSpec((tile, width), lambda j, s: (j, 0)),
                whole((1, width)), whole((1, width)),
            ],
            scratch_shapes=[pltpu.VMEM(rows, F32), pltpu.VMEM(rows, BF16), pltpu.VMEM(rows, F32)],
        ),
        out_shape=[
            jax.ShapeDtypeStruct(rows, BF16),
            *[jax.ShapeDtypeStruct((width, width), BF16)] * 4,
            jax.ShapeDtypeStruct((1, width), F32), jax.ShapeDtypeStruct((1, width), F32),
        ],
        compiler_params=pltpu.CompilerParams(vmem_limit_bytes=VMEM_BYTES),
        name="mix_back",
    )(facts, x, cot, g1, g2, mid, own, sib, normed, gated, *kept, half0, half0, half1, half1, *tables)


def ffn_kernel(nf_ref, gf_ref, wg_ref, wu_ref, wd_ref, h_ref, dg_ref, du_ref, gd_ref):
    nf, gf = nf_ref[...], gf_ref[...]
    g = mm(nf, wg_ref[...])
    u = mm(nf, wu_ref[...])
    dh = mm_nt(gf, wd_ref[...])
    sig = 1.0 / (1.0 + jnp.exp(-g))
    silu = g * sig
    h = (silu * u).astype(BF16)
    h_ref[...] = h
    du_ref[...] = (dh * silu).astype(BF16)
    dg_ref[...] = (dh * u * (sig * (1.0 + g * (1.0 - sig)))).astype(BF16)
    gd_ref[...] = mm_tn(h, gf).astype(BF16)


def ffn(nf, gf, wg, wu, wd):
    tok, width = nf.shape
    units = wg.shape[1]
    tile = 256
    whole = pl.BlockSpec((tok, width), lambda j: (0, 0))
    tall = pl.BlockSpec((width, tile), lambda j: (0, j))
    flat = pl.BlockSpec((tile, width), lambda j: (j, 0))
    column = pl.BlockSpec((tok, tile), lambda j: (0, j))
    return pl.pallas_call(
        ffn_kernel,
        grid=(units // tile,),
        in_specs=[whole, whole, tall, tall, flat],
        out_specs=[column, column, column, flat],
        out_shape=[
            *[jax.ShapeDtypeStruct((tok, units), BF16)] * 3,
            jax.ShapeDtypeStruct((units, width), BF16),
        ],
        compiler_params=pltpu.CompilerParams(vmem_limit_bytes=VMEM_BYTES),
        name="ffn",
    )(nf, gf, wg, wu, wd)


class Links:
    def __init__(self):
        self.wide = lax.axis_size("wide")
        self.narrow = lax.axis_size("narrow")
        self.core = lax.axis_index("wide") % 2
        self.outer = self.wide // 2
        place = lax.axis_index("wide")
        spot = lax.axis_index("narrow")
        self.bits = []
        span = self.outer
        while span > 1:
            span //= 2
            self.bits.append(("wide", self.wide, 2 * span, (place // (2 * span)) % 2))
        self.outer_bits = len(self.bits)
        span = self.narrow
        while span > 1:
            span //= 2
            self.bits.append(("narrow", self.narrow, span, (spot // span) % 2))

    def chain(self, turn):
        rest = list(range(1, len(self.bits)))
        turn %= len(rest)
        return [0] + rest[turn:] + rest[:turn]

    def swap_core(self, values):
        return lax.ppermute(values, "wide", [(i, i ^ 1) for i in range(self.wide)])

    def exchange(self, values, p):
        axis, size, stride, _ = self.bits[p]
        return lax.ppermute(values, axis, [(i, i ^ stride) for i in range(size)])

    def split(self, p, have, middle, rows):
        before = 2 ** sum(q < p for q in have)
        after = 2 ** sum(q > p for q in have)
        if p < self.outer_bits:
            return before, after * middle * rows
        return before * middle, after * rows

    def gather_step(self, block, p, have, middle):
        rows = block.shape[0] // (middle * 2 ** len(have))
        before, after = self.split(p, have, middle, rows)
        mine = block.reshape(before, 1, after, block.shape[1])
        other = self.exchange(block, p).reshape(mine.shape)
        bit = self.bits[p][3]
        both = jnp.where(
            bit == 0, jnp.concatenate([mine, other], axis=1), jnp.concatenate([other, mine], axis=1)
        )
        return both.reshape(-1, block.shape[1])

    def scatter_step(self, block, p, have, middle):
        rows = block.shape[0] // (middle * 2 ** len(have))
        before, after = self.split(p, have - {p}, middle, rows)
        parts = block.reshape(before, 2, after, block.shape[1])
        bit = self.bits[p][3]
        sent = lax.dynamic_index_in_dim(parts, 1 - bit, 1, keepdims=False)
        kept = lax.dynamic_index_in_dim(parts, bit, 1, keepdims=False)
        sent = sent.reshape(-1, block.shape[1])
        total = kept.reshape(sent.shape).astype(F32) + self.exchange(sent, p).astype(F32)
        return total.astype(BF16)

    def gather(self, blocks, chains, middles):
        have = [set() for _ in blocks]
        for k in range(len(self.bits)):
            for i, chain in enumerate(chains):
                blocks[i] = self.gather_step(blocks[i], chain[k], have[i], middles[i])
                have[i] = have[i] | {chain[k]}
        return blocks

    def scatter(self, blocks, chains, middles):
        have = [set(chain) for chain in chains]
        for k in reversed(range(len(self.bits))):
            for i, chain in enumerate(chains):
                blocks[i] = self.scatter_step(blocks[i], chain[k], have[i], middles[i])
                have[i] = have[i] - {chain[k]}
        return blocks


def unit_order(width, chunk):
    columns = np.arange(width)
    pairs = width // (2 * chunk)
    source = np.concatenate(
        [np.concatenate([(2 * i + core) * chunk + np.arange(chunk) for i in range(pairs)]) for core in range(2)]
    )
    return (columns[:, None] == source[None, :]).astype(ml_dtypes.bfloat16)


def on_device(tokens, cotangent, w_in, w_out, w_gu, w_down, gain_mix, gain_ffn, buckets, lengths):
    links = Links()
    core = links.core
    tok, width = tokens.shape
    rows = w_in.shape[0]
    ff = w_gu.shape[1] // 2
    units = ff // 2
    lanes = 128
    half_width = 2 * width + lanes

    tables = [jnp.asarray(t) for t in transform_tables(tok)]
    order = jnp.asarray(unit_order(width, ff // links.wide))
    facts = jnp.concatenate([buckets, lengths[0]]).astype(jnp.int32)

    gains = jnp.pad(jnp.stack([gain_mix, gain_ffn], axis=1), ((0, 0), (0, lanes - 2)))
    half0 = jnp.concatenate([w_in[:, : 2 * width], gains], axis=1)
    half1 = jnp.concatenate([w_in[:, 2 * width :], w_out, gains], axis=1)
    sorted_gu = mm(w_gu.reshape(rows * (2 * ff // width), width), order).astype(BF16)
    sorted_gu = sorted_gu.reshape(rows, 2 * ff // width, 2, width // 2)
    gu0 = sorted_gu[:, :, 0].reshape(rows, 2 * units)
    gu1 = sorted_gu[:, :, 1].reshape(rows, 2 * units)
    pack0 = jnp.concatenate([half0, gu0], axis=1)
    pack1 = jnp.concatenate([half1, gu1], axis=1)
    mine = jnp.where(core == 0, pack0, pack1)
    other = links.swap_core(jnp.where(core == 0, pack1, pack0))
    block = jnp.where(
        core == 0, jnp.concatenate([mine, other], axis=0), jnp.concatenate([other, mine], axis=0)
    )
    cuts = (0, 512, 1024, half_width)
    mixer_parts = [block[:, a:b] for a, b in zip(cuts[:-1], cuts[1:])]
    mixer_chains = [links.chain(i) for i in range(3)]
    mixer_parts = links.gather(mixer_parts, mixer_chains, [2, 2, 2])
    mixer_half = jnp.concatenate(mixer_parts, axis=1)
    mixer_sib = links.swap_core(mixer_half)
    full0 = jnp.where(core == 0, mixer_half, mixer_sib)
    full1 = jnp.where(core == 0, mixer_sib, mixer_half)
    gain_rows = full0[:, 2 * width : 2 * width + 2].astype(F32).T
    g1, g2 = gain_rows[0:1], gain_rows[1:2]

    ffn_parts = [block[:, half_width : half_width + units], block[:, half_width + units :], w_down]
    ffn_chains = [links.chain(i) for i in range(3)]
    middles = [2, 2, 1]
    wg, wu, wd = links.gather(ffn_parts, ffn_chains, middles)

    normed, gated, mid, nf, t, s, mixed, kf, vf, norms = mix_forward(facts, tokens, g1, g2, full0, full1, tables)

    mask = pad_mask(facts[0], [facts[1 + i] for i in range(ROW_SLOTS)], (tok, 1), tok)
    gf = (cotangent.astype(F32) * mask).astype(BF16)
    gf2 = jnp.concatenate([gf, links.swap_core(gf)], axis=0)
    nf2 = jnp.concatenate([nf, links.swap_core(nf)], axis=0)
    h, dg, du, grad_down = ffn(nf2, gf2, wg, wu, wd)
    grad_gate = mm_tn(nf2, dg).astype(BF16)
    grad_up = mm_tn(nf2, du).astype(BF16)
    dnf = mm_nt(dg, wg) + mm_nt(du, wu)
    dnf_sib = links.swap_core(dnf[tok:].astype(BF16))
    out = mm(h, wd)
    out_sib = links.swap_core(out[tok:].astype(BF16))
    layer_out = ((mid + out[:tok] + out_sib.astype(F32)) * mask).astype(BF16)

    sum_gate, sum_up, sum_down = links.scatter([grad_gate, grad_up, grad_down], ffn_chains, middles)

    grad_tokens, ga, gc, gv, go, gain1, gain2 = mix_back(
        facts, tokens, cotangent, g1, g2, mid, dnf[:tok], dnf_sib, normed, gated, (t, s, mixed, kf, vf), full0, full1, tables
    )
    devices = links.wide * links.narrow
    extras = jnp.concatenate([gain1, gain2, norms * (1.0 / devices)], axis=0).T.astype(BF16)
    extras = jnp.pad(extras, ((0, 0), (0, lanes - 3)))
    grad0 = jnp.concatenate([ga, gc, extras], axis=1)
    grad1 = jnp.concatenate([gv, go, extras * 0], axis=1)
    kept = jnp.where(core == 0, grad0, grad1)
    got = links.swap_core(jnp.where(core == 0, grad1, grad0))
    grad_half = (kept.astype(F32) + got.astype(F32)).astype(BF16)
    grad_parts = [grad_half[:, a:b] for a, b in zip(cuts[:-1], cuts[1:])]
    grad_parts = links.scatter(grad_parts, mixer_chains, [2, 2, 2])

    final = jnp.concatenate([*grad_parts, sum_gate, sum_up], axis=1).reshape(2, rows, half_width + 2 * units)
    own = lax.dynamic_index_in_dim(final, core, 0, keepdims=False)
    far = links.swap_core(lax.dynamic_index_in_dim(final, 1 - core, 0, keepdims=False))
    first = jnp.where(core == 0, own, far)
    second = jnp.where(core == 0, far, own)
    grad_w_in = jnp.concatenate([first[:, : 2 * width], second[:, :width]], axis=1).astype(F32)
    grad_w_out = second[:, width : 2 * width].astype(F32)
    extra = first[:, 2 * width : half_width].astype(F32).T
    groups = 2 * ff // width
    gu_pair = jnp.concatenate(
        [
            first[:, half_width:].reshape(rows, groups, width // 2),
            second[:, half_width:].reshape(rows, groups, width // 2),
        ],
        axis=2,
    )
    grad_w_gu = mm_nt(gu_pair.reshape(rows * groups, width), order).reshape(rows, 2 * ff)
    return (
        layer_out, grad_tokens, grad_w_in, grad_w_out, grad_w_gu, sum_down.astype(F32), extra[0], extra[1], extra[2],
    )


def solution(mesh):
    both = ("wide", "narrow")
    flat, tall = P(both), P(both, None)
    return jax.shard_map(
        on_device,
        mesh=mesh,
        in_specs=(tall, tall, tall, tall, tall, tall, flat, flat, flat, tall),
        out_specs=(tall, tall, tall, tall, tall, tall, flat, flat, flat),
        check_vma=False,
    )
```

time: 1160 us -> 337 us (0.29)
  waiting for transfers between devices: 674 us -> 133 us
  matrix products: 188 us -> 18.4 us
  blocking collectives: 142 us -> 0 us
  starting transfers between devices: 0.44 us -> 55.6 us
  Pallas kernels: 0 us -> 53.8 us
  loops' own time: 53.2 us -> 0 us
  local copies, waits for them, and re-layouts: 51.2 us -> 19.7 us
  other arithmetic: 30.3 us -> 48.5 us
  between operations: 15.1 us -> 2.77 us
    unnamed x12 -> x0, waiting for transfers between devices: 421 us -> none
    dot_general x48 -> x8, matrix products: 188 us -> 18.4 us  [the longest x2 8.11 us: mm_tn(): lax.dot_general(left, right, (((0,), (0,)), ((), ())), preferred_element_...]
    reduce_scatter x6 -> x0, waiting for transfers between devices: 160 us -> none  [the longest x1 77.3 us: on_device(): lax.psum_scatter(part_gu.astype(jnp.bfloat16), 'wide', scatter_dimension=...]
    ppermute x0 -> x56, waiting for transfers between devices: none -> 133 us  [the longest x48 132 us: exchange(): return lax.ppermute(values, axis, [(i, i ^ stride) for i in range(size)])]
    unnamed x2 -> x0, blocking collectives: 101 us -> none
    all_gather x4 -> x0, waiting for transfers between devices: 93 us -> none  [the longest x1 53.3 us: on_device(): lax.all_gather(w_down, ('wide', 'narrow'), axis=0, tiled=True)]
    ppermute x0 -> x56, starting transfers between devices: none -> 55.6 us  [the longest x48 54.2 us: exchange(): return lax.ppermute(values, axis, [(i, i ^ stride) for i in range(size)])]
    pallas_call x0 -> x3, Pallas kernels: none -> 53.8 us  [the longest x1 22.3 us: mix_back(): pl.pallas_call(mix_back_kernel, grid_spec=pltpu.PrefetchScalarGridSpec(nu...]
  transfers between devices with their start and end apart: 11 -> 56, of which waited for: 7 -> 29; matrix products, arithmetic and copies ran while one was open for 13% -> 18% of each run, Pallas kernels for 0% -> 12%
where the time goes in v1:
time: 337 us; the launch traced here: 332 us
  waiting for transfers between devices  133 us (39%)
  starting transfers between devices  55.6 us (16%)
  Pallas kernels  53.8 us (16%)
  other arithmetic  48.5 us (14%)
  local copies, waits for them, and re-layouts  19.7 us (6%)
  matrix products  18.4 us (5%)
    ppermute x48, waiting for transfers between devices, exchange(): return lax.ppermute(values, axis, [(i, i ^ stride) for i in range(size)])  132 us
    ppermute x48, starting transfers between devices, exchange(): return lax.ppermute(values, axis, [(i, i ^ stride) for i in range(size)])  54.2 us
    pallas_call x1, Pallas kernels, mix_back(): pl.pallas_call(mix_back_kernel, grid_spec=pltpu.PrefetchScalarGridSpec(nu...  22.3 us
    select_n x29, other arithmetic, gather_step(): jnp.where(bit == 0, jnp.concatenate([mine, other], axis=1), jnp.concatena...  19.7 us
    pallas_call x1, Pallas kernels, mix_forward(): pl.pallas_call(mix_forward_kernel, grid_spec=pltpu.PrefetchScalarGridSpec...  16.5 us
    pallas_call x1, Pallas kernels, ffn(): pl.pallas_call(ffn_kernel, grid=(units // tile,), in_specs=[whole, whole,...  15 us
    dot_general x2, matrix products, mm_tn(): lax.dot_general(left, right, (((0,), (0,)), ((), ())), preferred_element_...  8.11 us
  transfers between devices with their start and end apart: 56, of which 29 were waited for; matrix products, arithmetic and copies ran while one was open for 18% of the time, Pallas kernels for 12%

profile of v1, /device:TPU:0, one launch (start us, length us, event | category | flops | bytes accessed | tf_op | source)
XLA Modules:
  0.0 331.8 jit_solution(8334064333280229821)
XLA Ops:
  4.5 3.7 %collective-permute-start.24 = (bf16[96,768]{1,0:T(8,128)(2,1)S(1)}, bf16[96,768]{1,0:T(8,128)(2,1)S(1)}, u32[]{:S(2)}, u32[]{:S(2)}) collective-permute-start(bf16[96,768]{1,0:T(8,128)(2,1)S(1)} %copy-done.23), channel_id=1, source_target_pairs={{0,16},{2,18},{4,20},{6,22},{8,24},{10,26},{12,28},{14,30},{16,0},... | collective-permute-start | bytes 442376 | tf_op jit(solution)/shard_map/ppermute | solution.py:376
  12.5 3.3 collective-permute-done.24
  35.9 3.5 %collective-permute-done.7 = bf16[192,512]{1,0:T(8,128)(2,1)S(1)} collective-permute-done((bf16[192,512]{1,0:T(8,128)(2,1)S(1)}, bf16[192,512]{1,0:T(8,128)(2,1)S(1)}, u32[]{:S(2)}, u32[]{:S(2)}) %collective-permute-start.7) | collective-permute-done | bytes 196640 | tf_op jit(solution)/shard_map/ppermute | solution.py:376
  43.6 6.5 %collective-permute-done.4 = bf16[384,512]{1,0:T(8,128)(2,1)S(1)} collective-permute-done((bf16[384,512]{1,0:T(8,128)(2,1)S(1)}, bf16[384,512]{1,0:T(8,128)(2,1)S(1)}, u32[]{:S(2)}, u32[]{:S(2)}) %collective-permute-start.4) | collective-permute-done | bytes 393248 | tf_op jit(solution)/shard_map/ppermute | solution.py:376
  55.3 7.1 %collective-permute-done.20 = bf16[48,1536]{1,0:T(8,128)(2,1)S(1)} collective-permute-done((bf16[48,1536]{1,0:T(8,128)(2,1)S(1)}, bf16[48,1536]{1,0:T(8,128)(2,1)S(1)}, u32[]{:S(2)}, u32[]{:S(2)}) %collective-permute-start.20) | collective-permute-done | bytes 147488 | tf_op jit(solution)/shard_map/ppermute | solution.py:376
  71.0 9.4 %collective-permute-done.26 = bf16[384,768]{1,0:T(8,128)(2,1)S(1)} collective-permute-done((bf16[384,768]{1,0:T(8,128)(2,1)S(1)}, bf16[384,768]{1,0:T(8,128)(2,1)S(1)}, u32[]{:S(2)}, u32[]{:S(2)}) %collective-permute-start.26) | collective-permute-done | bytes 589856 | tf_op jit(solution)/shard_map/ppermute | solution.py:376
  91.4 24.4 %collective-permute-done.18 = bf16[192,1536]{1,0:T(8,128)(2,1)} collective-permute-done((bf16[192,1536]{1,0:T(8,128)(2,1)}, bf16[192,1536]{1,0:T(8,128)(2,1)}, u32[]{:S(2)}, u32[]{:S(2)}) %collective-permute-start.18) | collective-permute-done | bytes 589856 | tf_op jit(solution)/shard_map/ppermute | solution.py:376
  120.2 3.5 %maximum_select_fusion.2 = bf16[4,2,192,768]{3,2,1,0:T(8,128)(2,1)} fusion(bf16[4,1,192,768]{3,2,1,0:T(8,128)(2,1)} %bitcast.95, bf16[4,1,192,768]{3,2,1,0:T(8,128)(2,1)S(1)} %bitcast.307, pred[]{:T(512)S(6)} %eq.84), kind=kLoop, calls=%fused_computation.11 | loop fusion | flops 3538944 | bytes 4718593 | tf_op jit(solution)/shard_map/jit(_where)/select_n | solution.py:391
  123.7 3.9 %broadcast_select_fusion.1 = (bf16[768,1664]{1,0:T(8,128)(2,1)}, bf16[768,1664]{1,0:T(8,128)(2,1)S(1)}) fusion(bf16[768,1664]{1,0:T(8,128)(2,1)} %collective-permute-done.13, pred[]{:T(512)S(6)} %eq.82, bf16[768,640]{1,0:T(8,128)(2,1)S(1)} %bitcast.301, bf16[768,512]{1,0:T(8,128)(2,1)S(1)} %bitcast.305, bf16[768,512]{1,0:T(8,128)(2,1)S(1)} %bitcast.303), kind=kLoop, calls=%fused_computation.7 | loop fusion | flops 10223616 | bytes 10223617 | tf_op jit(solution)/shard_map/jit(_where)/select_n | solution.py:468
  129.6 16.5 %mix_forward.1 = (bf16[512,768]{1,0:T(8,128)(2,1)}, bf16[512,768]{1,0:T(8,128)(2,1)}, f32[512,768]{1,0:T(8,128)}, bf16[512,768]{1,0:T(8,128)(2,1)}, f32[512,768]...) custom-call(s32[5]{0:T(128)} %pad_add_fusion.facts, ...), custom_call_target="tpu_custom_call" | custom-call | tf_op jit(solution)/shard_map/mix_forward/pallas_call | solution.py:163
  146.2 4.5 %maximum_select_fusion.1 = bf16[2,2,192,1536]{3,2,1,0:T(8,128)(2,1)} fusion(bf16[2,1,192,1536]{3,2,1,0:T(8,128)(2,1)} %bitcast.80, bf16[2,1,192,1536]{3,2,1,0:T(8,128)(2,1)} %bitcast.77, pred[]{:T(512)S(6)} %eq.85), kind=kLoop, calls=%fused_computation.10 | loop fusion | flops 3538944 | bytes 4718593 | tf_op jit(solution)/shard_map/jit(_where)/select_n | solution.py:391
  150.7 4.3 %maximum_select_fusion = bf16[16,2,24,1536]{3,2,1,0:T(8,128)(2,1)} fusion(bf16[16,1,24,1536]{3,2,1,0:T(8,128)(2,1)} %bitcast.65, bf16[16,1,24,1536]{3,2,1,0:T(8,128)(2,1)} %bitcast.62, pred[]{:T(512)S(6)} %eq.83), kind=kLoop, calls=%fused_computation.9 | loop fusion | flops 3538944 | bytes 4718593 | tf_op jit(solution)/shard_map/jit(_where)/select_n | solution.py:391
  156.3 15.0 %ffn.1 = (bf16[1024,1536]{1,0:T(8,128)(2,1)}, bf16[1024,1536]{1,0:T(8,128)(2,1)}, bf16[1024,1536]{1,0:T(8,128)(2,1)}, bf16[1536,768]{1,0:T(8,128)(2,1)}) custom-call(bf16[1024,768]{1,0:T(8,128)(2,1)} %copy-done.13, bf16[1024,768]{1,0:T(8,128)(2,1)} %pad_maximum_fusion.3.gf_ref, bf16[768,1536]{1,0:T(8,128)(2,1)} %bitcast.298, bf16[768,1536]{1,0:T(8,128)(2,1)} %bitcast.296, ...), custom_call_target="tpu_custom_call" | custom-call | tf_op jit(solution)/shard_map/ffn/pallas_call | solution.py:333
  171.4 5.2 %convolution_convert_fusion = bf16[768,1536]{1,0:T(8,128)(2,1)S(1)} fusion(bf16[1024,768]{1,0:T(8,128)(2,1)} %copy-done.13, bf16[1024,1536]{1,0:T(8,128)(2,1)} %get-tuple-element.34), kind=kOutput, calls=%fused_computation.1 | convolution fusion | flops 2417098752 | bytes 7077888 | tf_op jit(solution)/shard_map/dot_general | solution.py:51
  199.5 22.3 %mix_back.1 = (bf16[512,768]{1,0:T(8,128)(2,1)}, bf16[768,768]{1,0:T(8,128)(2,1)}, bf16[768,768]{1,0:T(8,128)(2,1)}, bf16[768,768]{1,0:T(8,128)(2,1)}, bf16[768,...) custom-call(s32[5]{0:T(128)} %pad_add_fusion.facts, bf16[512,768]{1,0:T(8,128)(2,1)} %x_ref.3, ...), custom_call_target="tpu_custom_call" | custom-call | tf_op jit(solution)/shard_map/mix_back/pallas_call | solution.py:280
  239.6 8.5 %collective-permute-done.53 = bf16[384,768]{1,0:T(8,128)(2,1)S(1)} collective-permute-done((bf16[384,768]{1,0:T(8,128)(2,1)S(1)}, bf16[384,768]{1,0:T(8,128)(2,1)S(1)}, u32[]{:S(2)}, u32[]{:S(2)}) %collective-permute-start.53) | collective-permute-done | bytes 589856 | tf_op jit(solution)/shard_map/ppermute | solution.py:376
  251.8 3.5 %collective-permute-done.44 = bf16[192,1536]{1,0:T(8,128)(2,1)S(1)} collective-permute-done((bf16[192,1536]{1,0:T(8,128)(2,1)S(1)}, bf16[192,1536]{1,0:T(8,128)(2,1)S(1)}, u32[]{:S(2)}, u32[]{:S(2)}) %collective-permute-start.44) | collective-permute-done | bytes 589856 | tf_op jit(solution)/shard_map/ppermute | solution.py:376
  267.0 4.0 %collective-permute-start.46 = (bf16[48,1536]{1,0:T(8,128)(2,1)S(1)}, bf16[48,1536]{1,0:T(8,128)(2,1)S(1)}, u32[]{:S(2)}, u32[]{:S(2)}) collective-permute-start(bf16[48,1536]{1,0:T(8,128)(2,1)S(1)} %dynamic-slice_bitcast_fusion.3), channel_id=1, source_target_pairs={{0,16},{2,18},{4,20},{6,22},{8,24},{10,26},{12,28},{14,30},{16,0},... | collective-permute-start | bytes 442376 | tf_op jit(solution)/shard_map/ppermute | solution.py:376
  271.4 8.9 %collective-permute-done.35 = bf16[384,512]{1,0:T(8,128)(2,1)S(1)} collective-permute-done((bf16[384,512]{1,0:T(8,128)(2,1)S(1)}, bf16[384,512]{1,0:T(8,128)(2,1)S(1)}, u32[]{:S(2)}, u32[]{:S(2)}) %collective-permute-start.35) | collective-permute-done | bytes 393248 | tf_op jit(solution)/shard_map/ppermute | solution.py:376
  281.1 10.6 %collective-permute-done.39 = bf16[384,640]{1,0:T(8,128)(2,1)S(1)} collective-permute-done((bf16[384,640]{1,0:T(8,128)(2,1)S(1)}, bf16[384,640]{1,0:T(8,128)(2,1)S(1)}, u32[]{:S(2)}, u32[]{:S(2)}) %collective-permute-start.39) | collective-permute-done | bytes 491552 | tf_op jit(solution)/shard_map/ppermute | solution.py:376
  292.4 6.1 %collective-permute-done.32 = bf16[192,512]{1,0:T(8,128)(2,1)S(1)} collective-permute-done((bf16[192,512]{1,0:T(8,128)(2,1)S(1)}, bf16[192,512]{1,0:T(8,128)(2,1)S(1)}, u32[]{:S(2)}, u32[]{:S(2)}) %collective-permute-start.32) | collective-permute-done | bytes 196640 | tf_op jit(solution)/shard_map/ppermute | solution.py:376
  298.8 4.3 %collective-permute-done.37 = bf16[96,512]{1,0:T(8,128)(2,1)S(1)} collective-permute-done((bf16[96,512]{1,0:T(8,128)(2,1)S(1)}, bf16[96,512]{1,0:T(8,128)(2,1)S(1)}, u32[]{:S(2)}, u32[]{:S(2)}) %collective-permute-start.37) | collective-permute-done | bytes 98336 | tf_op jit(solution)/shard_map/ppermute | solution.py:376
  303.1 5.1 %collective-permute-done.33 = bf16[96,512]{1,0:T(8,128)(2,1)S(1)} collective-permute-done((bf16[96,512]{1,0:T(8,128)(2,1)S(1)}, bf16[96,512]{1,0:T(8,128)(2,1)S(1)}, u32[]{:S(2)}, u32[]{:S(2)}) %collective-permute-start.33) | collective-permute-done | bytes 98336 | tf_op jit(solution)/shard_map/ppermute | solution.py:376
  321.5 4.3 %collective-permute-done.42 = bf16[48,640]{1,0:T(8,128)(2,1)S(1)} collective-permute-done((bf16[48,640]{1,0:T(8,128)(2,1)S(1)}, bf16[48,640]{1,0:T(8,128)(2,1)S(1)}, u32[]{:S(2)}, u32[]{:S(2)}) %collective-permute-start.42) | collective-permute-done | bytes 61472 | tf_op jit(solution)/shard_map/ppermute | solution.py:376
  (296 shorter events, 140.8 us)
Async XLA Ops:
  12.2 74.2 %collective-permute-start.15 = (bf16[512,768]{1,0:T(8,128)(2,1)S(1)}, bf16[512,768]{1,0:T(8,128)(2,1)}, u32[]{:S(2)}, u32[]{:S(2)}) collective-permute-start(bf16[512,768]{1,0:T(8,128)(2,1)S(1)} %multiply_convert_fusion), channel_id=1, source_target_pairs={{0,2},{2,0},{4,6},{6,4},{8,10},{10,8},{12,14},{14,12},{16,18},{18,... | collective-permute-start | bytes 2359304 | tf_op jit(solution)/shard_map/ppermute | solution.py:372
  33.7 30.3 %collective-permute-start.25 = (bf16[192,768]{1,0:T(8,128)(2,1)S(1)}, bf16[192,768]{1,0:T(8,128)(2,1)S(1)}, u32[]{:S(2)}, u32[]{:S(2)}) collective-permute-start(bf16[192,768]{1,0:T(8,128)(2,1)S(1)} %bitcast.382), channel_id=1, source_target_pairs={{0,1},{1,0},{2,3},{3,2},{4,5},{5,4},{6,7},{7,6},{8,9},{9,8},{10,11... | collective-permute-start | bytes 884744 | tf_op jit(solution)/shard_map/ppermute | solution.py:376
  35.3 14.7 %collective-permute-start.4 = (bf16[384,512]{1,0:T(8,128)(2,1)S(1)}, bf16[384,512]{1,0:T(8,128)(2,1)S(1)}, u32[]{:S(2)}, u32[]{:S(2)}) collective-permute-start(bf16[384,512]{1,0:T(8,128)(2,1)S(1)} %bitcast.329), channel_id=1, source_target_pairs={{0,1},{1,0},{2,3},{3,2},{4,5},{5,4},{6,7},{7,6},{8,9},{9,8},{10,11... | collective-permute-start | bytes 1179656 | tf_op jit(solution)/shard_map/ppermute | solution.py:376
  55.3 68.5 %collective-permute-start.13 = (bf16[768,1664]{1,0:T(8,128)(2,1)}, bf16[768,1664]{1,0:T(8,128)(2,1)}, u32[]{:S(2)}, u32[]{:S(2)}) collective-permute-start(bf16[768,1664]{1,0:T(8,128)(2,1)} %pad_maximum_fusion), channel_id=1, source_target_pairs={{0,2},{2,0},{4,6},{6,4},{8,10},{10,8},{12,14},{14,12},{16,18},{18,... | collective-permute-start | bytes 7667720 | tf_op jit(solution)/shard_map/ppermute | solution.py:372
  64.0 16.3 %collective-permute-start.26 = (bf16[384,768]{1,0:T(8,128)(2,1)S(1)}, bf16[384,768]{1,0:T(8,128)(2,1)S(1)}, u32[]{:S(2)}, u32[]{:S(2)}) collective-permute-start(bf16[384,768]{1,0:T(8,128)(2,1)S(1)} %bitcast.319), channel_id=1, source_target_pairs={{0,8},{2,10},{4,12},{6,14},{8,0},{10,2},{12,4},{14,6},{16,24},{18,... | collective-permute-start | bytes 1769480 | tf_op jit(solution)/shard_map/ppermute | solution.py:376
  64.4 19.1 %collective-permute-start.17 = (bf16[96,1536]{1,0:T(8,128)(2,1)S(1)}, bf16[96,1536]{1,0:T(8,128)(2,1)S(1)}, u32[]{:S(2)}, u32[]{:S(2)}) collective-permute-start(bf16[96,1536]{1,0:T(8,128)(2,1)S(1)} %bitcast.383), channel_id=1, source_target_pairs={{0,8},{2,10},{4,12},{6,14},{8,0},{10,2},{12,4},{14,6},{16,24},{18,... | collective-permute-start | bytes 884744 | tf_op jit(solution)/shard_map/ppermute | solution.py:376
  69.4 19.5 %collective-permute-start.22 = (bf16[192,1536]{1,0:T(8,128)(2,1)S(1)}, bf16[192,1536]{1,0:T(8,128)(2,1)}, u32[]{:S(2)}, u32[]{:S(2)}) collective-permute-start(bf16[192,1536]{1,0:T(8,128)(2,1)S(1)} %bitcast.317), channel_id=1, source_target_pairs={{0,1},{1,0},{2,3},{3,2},{4,5},{5,4},{6,7},{7,6},{8,9},{9,8},{10,11... | collective-permute-start | bytes 1769480 | tf_op jit(solution)/shard_map/ppermute | solution.py:376
  80.5 39.7 %collective-permute-start.27 = (bf16[768,768]{1,0:T(8,128)(2,1)S(1)}, bf16[768,768]{1,0:T(8,128)(2,1)}, u32[]{:S(2)}, u32[]{:S(2)}) collective-permute-start(bf16[768,768]{1,0:T(8,128)(2,1)S(1)} %bitcast.306), channel_id=1, source_target_pairs={{0,4},{2,6},{4,0},{6,2},{8,12},{10,14},{12,8},{14,10},{16,20},{18,... | collective-permute-start | bytes 3538952 | tf_op jit(solution)/shard_map/ppermute | solution.py:376
  84.4 31.4 %collective-permute-start.18 = (bf16[192,1536]{1,0:T(8,128)(2,1)}, bf16[192,1536]{1,0:T(8,128)(2,1)}, u32[]{:S(2)}, u32[]{:S(2)}) collective-permute-start(bf16[192,1536]{1,0:T(8,128)(2,1)} %bitcast.59), channel_id=1, source_target_pairs={{0,4},{2,6},{4,0},{6,2},{8,12},{10,14},{12,8},{14,10},{16,20},{18,... | collective-permute-start | bytes 1769480 | tf_op jit(solution)/shard_map/ppermute | solution.py:376
  91.4 54.8 %collective-permute-start.23 = (bf16[384,1536]{1,0:T(8,128)(2,1)}, bf16[384,1536]{1,0:T(8,128)(2,1)}, u32[]{:S(2)}, u32[]{:S(2)}) collective-permute-start(bf16[384,1536]{1,0:T(8,128)(2,1)} %bitcast.78), channel_id=1, source_target_pairs={{0,8},{2,10},{4,12},{6,14},{8,0},{10,2},{12,4},{14,6},{16,24},{18,... | collective-permute-start | bytes 3538952 | tf_op jit(solution)/shard_map/ppermute | solution.py:376
  118.6 32.1 %collective-permute-start.19 = (bf16[384,1536]{1,0:T(8,128)(2,1)}, bf16[384,1536]{1,0:T(8,128)(2,1)}, u32[]{:S(2)}, u32[]{:S(2)}) collective-permute-start(bf16[384,1536]{1,0:T(8,128)(2,1)} %bitcast.63), channel_id=1, source_target_pairs={{0,1},{1,0},{2,3},{3,2},{4,5},{5,4},{6,7},{7,6},{8,9},{9,8},{10,11... | collective-permute-start | bytes 3538952 | tf_op jit(solution)/shard_map/ppermute | solution.py:376
  185.3 45.8 %collective-permute-start.52 = (bf16[768,768]{1,0:T(8,128)(2,1)}, bf16[768,768]{1,0:T(8,128)(2,1)}, u32[]{:S(2)}, u32[]{:S(2)}) collective-permute-start(bf16[768,768]{1,0:T(8,128)(2,1)} %bitcast.165), channel_id=1, source_target_pairs={{0,4},{2,6},{4,0},{6,2},{8,12},{10,14},{12,8},{14,10},{16,20},{18,... | collective-permute-start | bytes 3538952 | tf_op jit(solution)/shard_map/ppermute | solution.py:376
  188.3 46.0 %collective-permute-start.47 = (bf16[384,1536]{1,0:T(8,128)(2,1)}, bf16[384,1536]{1,0:T(8,128)(2,1)}, u32[]{:S(2)}, u32[]{:S(2)}) collective-permute-start(bf16[384,1536]{1,0:T(8,128)(2,1)} %bitcast.150), channel_id=1, source_target_pairs={{0,8},{2,10},{4,12},{6,14},{8,0},{10,2},{12,4},{14,6},{16,24},{18,... | collective-permute-start | bytes 3538952 | tf_op jit(solution)/shard_map/ppermute | solution.py:376
  193.8 34.2 %collective-permute-start.28 = (bf16[512,768]{1,0:T(8,128)(2,1)}, bf16[512,768]{1,0:T(8,128)(2,1)}, u32[]{:S(2)}, u32[]{:S(2)}) collective-permute-start(bf16[512,768]{1,0:T(8,128)(2,1)} %slice.183), channel_id=1, source_target_pairs={{0,2},{2,0},{4,6},{6,4},{8,10},{10,8},{12,14},{14,12},{16,18},{18,... | collective-permute-start | bytes 2359304 | tf_op jit(solution)/shard_map/ppermute | solution.py:372
  198.2 39.5 %collective-permute-start.43 = (bf16[384,1536]{1,0:T(8,128)(2,1)}, bf16[384,1536]{1,0:T(8,128)(2,1)}, u32[]{:S(2)}, u32[]{:S(2)}) collective-permute-start(bf16[384,1536]{1,0:T(8,128)(2,1)} %bitcast.138), channel_id=1, source_target_pairs={{0,1},{1,0},{2,3},{3,2},{4,5},{5,4},{6,7},{7,6},{8,9},{9,8},{10,11... | collective-permute-start | bytes 3538952 | tf_op jit(solution)/shard_map/ppermute | solution.py:376
  227.8 37.6 %collective-permute-start.30 = (bf16[768,1664]{1,0:T(8,128)(2,1)S(1)}, bf16[768,1664]{1,0:T(8,128)(2,1)S(1)}, u32[]{:S(2)}, u32[]{:S(2)}) collective-permute-start(bf16[768,1664]{1,0:T(8,128)(2,1)S(1)} %broadcast_select_fusion), channel_id=1, source_target_pairs={{0,2},{2,0},{4,6},{6,4},{8,10},{10,8},{12,14},{14,12},{16,18},{18,... | collective-permute-start | bytes 7667720 | tf_op jit(solution)/shard_map/ppermute | solution.py:372
  232.8 15.3 %collective-permute-start.53 = (bf16[384,768]{1,0:T(8,128)(2,1)S(1)}, bf16[384,768]{1,0:T(8,128)(2,1)S(1)}, u32[]{:S(2)}, u32[]{:S(2)}) collective-permute-start(bf16[384,768]{1,0:T(8,128)(2,1)S(1)} %bitcast.355), channel_id=1, source_target_pairs={{0,8},{2,10},{4,12},{6,14},{8,0},{10,2},{12,4},{14,6},{16,24},{18,... | collective-permute-start | bytes 1769480 | tf_op jit(solution)/shard_map/ppermute | solution.py:376
  236.0 15.2 %collective-permute-start.48 = (bf16[192,1536]{1,0:T(8,128)(2,1)S(1)}, bf16[192,1536]{1,0:T(8,128)(2,1)S(1)}, u32[]{:S(2)}, u32[]{:S(2)}) collective-permute-start(bf16[192,1536]{1,0:T(8,128)(2,1)S(1)} %bitcast.356), channel_id=1, source_target_pairs={{0,1},{1,0},{2,3},{3,2},{4,5},{5,4},{6,7},{7,6},{8,9},{9,8},{10,11... | collective-permute-start | bytes 1769480 | tf_op jit(solution)/shard_map/ppermute | solution.py:376
  239.3 16.0 %collective-permute-start.44 = (bf16[192,1536]{1,0:T(8,128)(2,1)S(1)}, bf16[192,1536]{1,0:T(8,128)(2,1)S(1)}, u32[]{:S(2)}, u32[]{:S(2)}) collective-permute-start(bf16[192,1536]{1,0:T(8,128)(2,1)S(1)} %bitcast.357), channel_id=1, source_target_pairs={{0,4},{2,6},{4,0},{6,2},{8,12},{10,14},{12,8},{14,10},{16,20},{18,... | collective-permute-start | bytes 1769480 | tf_op jit(solution)/shard_map/ppermute | solution.py:376
  257.2 68.9 %collective-permute-start.55 = (bf16[96,768]{1,0:T(8,128)(2,1)S(1)}, bf16[96,768]{1,0:T(8,128)(2,1)S(1)}, u32[]{:S(2)}, u32[]{:S(2)}) collective-permute-start(bf16[96,768]{1,0:T(8,128)(2,1)S(1)} %dynamic-slice_bitcast_fusion.1), channel_id=1, source_target_pairs={{0,16},{2,18},{4,20},{6,22},{8,24},{10,26},{12,28},{14,30},{16,0},... | collective-permute-start | bytes 442376 | tf_op jit(solution)/shard_map/ppermute | solution.py:376
  260.2 65.7 %collective-permute-start.50 = (bf16[48,1536]{1,0:T(8,128)(2,1)S(1)}, bf16[48,1536]{1,0:T(8,128)(2,1)S(1)}, u32[]{:S(2)}, u32[]{:S(2)}) collective-permute-start(bf16[48,1536]{1,0:T(8,128)(2,1)S(1)} %dynamic-slice_bitcast_fusion.2), channel_id=1, source_target_pairs={{0,16},{2,18},{4,20},{6,22},{8,24},{10,26},{12,28},{14,30},{16,0},... | collective-permute-start | bytes 442376 | tf_op jit(solution)/shard_map/ppermute | solution.py:376
  266.9 13.4 %collective-permute-start.35 = (bf16[384,512]{1,0:T(8,128)(2,1)S(1)}, bf16[384,512]{1,0:T(8,128)(2,1)S(1)}, u32[]{:S(2)}, u32[]{:S(2)}) collective-permute-start(bf16[384,512]{1,0:T(8,128)(2,1)S(1)} %bitcast.376), channel_id=1, source_target_pairs={{0,8},{2,10},{4,12},{6,14},{8,0},{10,2},{12,4},{14,6},{16,24},{18,... | collective-permute-start | bytes 1179656 | tf_op jit(solution)/shard_map/ppermute | solution.py:376
  267.0 58.8 %collective-permute-start.46 = (bf16[48,1536]{1,0:T(8,128)(2,1)S(1)}, bf16[48,1536]{1,0:T(8,128)(2,1)S(1)}, u32[]{:S(2)}, u32[]{:S(2)}) collective-permute-start(bf16[48,1536]{1,0:T(8,128)(2,1)S(1)} %dynamic-slice_bitcast_fusion.3), channel_id=1, source_target_pairs={{0,16},{2,18},{4,20},{6,22},{8,24},{10,26},{12,28},{14,30},{16,0},... | collective-permute-start | bytes 442376 | tf_op jit(solution)/shard_map/ppermute | solution.py:376
  292.2 16.2 %collective-permute-start.40 = (bf16[192,640]{1,0:T(8,128)(2,1)S(1)}, bf16[192,640]{1,0:T(8,128)(2,1)S(1)}, u32[]{:S(2)}, u32[]{:S(2)}) collective-permute-start(bf16[192,640]{1,0:T(8,128)(2,1)S(1)} %bitcast.391), channel_id=1, source_target_pairs={{0,8},{2,10},{4,12},{6,14},{8,0},{10,2},{12,4},{14,6},{16,24},{18,... | collective-permute-start | bytes 737288 | tf_op jit(solution)/shard_map/ppermute | solution.py:376
  (66 other events, 422.1 us)
